TPU v7x, 32 devices: a whole 2x2x4 slice. The times are simulated.
32 devices in a mesh: blk: 8 (over y, x, core), dp: 4 (over z).
Axes of the slice: x: 2, y: 2, z: 4, core: 2. Of those that a mesh axis runs over, the one named last changes fastest.
Arguments:
- inputs: bfloat16 [4096, 2304], P(('blk', 'dp')), may hold values from -6 to 6
- queries: bfloat16 [4096, 2048], P(('blk', 'dp')), may hold values from -80 to 80
- keys: bfloat16 [4096, 1024], P(('blk', 'dp')), may hold values from -3.5 to 3.5
- grad_attn: bfloat16 [4096, 2048], P(('blk', 'dp')), may hold values from -6 to 6
- segment_ids: int32 [32, 128], P(('blk', 'dp')), may hold values from 0 to 7, never falling along the last dimension, each value on 1 to 32 neighbouring positions
- value_weight: bfloat16 [2304, 1024], P('blk'), may hold values from -0.125 to 0.125
Outputs:
- grad_inputs: bfloat16 [4096, 2304], P(('blk', 'dp'))
- grad_weight: float32 [2304, 1024], P('blk')
Inputs may be any that keep to these rules, and one draw needn't show every extreme that they name: `segment_ids`: within a history the basket numbers never fall; a basket holds 1 to 32 tokens.
All inputs are finite; a program needn't handle non-finite values.
Results may differ from a plain program's by a relative error of at most 0.0057.
Values may be sent and summed in bfloat16 or wider, within the bound.
A program may use at most 64 MiB of HBM per device.

v0:
```python
import math

import jax
import jax.numpy as jnp
from jax import lax
from jax.sharding import PartitionSpec as P

KV_HEADS = 8
GROUP = 2
HEAD_DIM = 128


query_scale = 1.0 / 12.0


def from_behind(value, axis, steps):
    count = lax.axis_size(axis)
    pairs = [(source, (source + steps) % count) for source in range(count)]
    return lax.ppermute(value, axis, pairs)


def value_gradient(queries, keys, grad_attn, segments):
    length = segments.shape[0]
    query_heads = queries.reshape(length, KV_HEADS, GROUP, HEAD_DIM)
    key_heads = keys.reshape(length, KV_HEADS, HEAD_DIM)
    scores = (
        jnp.einsum("tkgd,skd->kgts", query_heads, key_heads, preferred_element_type=jnp.float32)
        * query_scale
    )
    allowed = segments[None, :] <= segments[:, None]
    scores = jnp.where(allowed, scores, -jnp.inf)
    row_max = jnp.max(scores, axis=-1, keepdims=True)
    weights = jnp.exp(scores - row_max)
    attn_probs = (weights / jnp.sum(weights, axis=-1, keepdims=True)).astype(jnp.bfloat16)
    grad_heads = grad_attn.reshape(length, KV_HEADS, GROUP, HEAD_DIM)
    summed = jnp.einsum(
        "kgts,tkgd->skd", attn_probs, grad_heads, preferred_element_type=jnp.float32
    )
    return summed.reshape(length, KV_HEADS * HEAD_DIM).astype(jnp.bfloat16)


def local(inputs, queries, keys, grad_attn, segment_ids, value_weight):
    value_grad = value_gradient(queries, keys, grad_attn, segment_ids[0])
    shard_rows = value_weight.shape[0]
    local_tokens = inputs.shape[0]
    cycle_size = lax.axis_size("blk")
    cycle_index = lax.axis_index("blk")
    grad_inputs = lax.dot_general(
        value_grad,
        lax.all_gather(value_weight, "blk", axis=0, tiled=True),
        (((1,), (1,)), ((), ())),
        preferred_element_type=jnp.float32,
    ).astype(jnp.bfloat16)

    def owner_term(owner):
        columns = lax.dynamic_slice_in_dim(inputs, owner * shard_rows, shard_rows, 1)
        return lax.dot_general(
            columns, value_grad, (((0,), (0,)), ((), ())), preferred_element_type=jnp.float32
        )

    def single_step(cycle_step, carried):
        return from_behind(carried, "blk", 1) + owner_term(
            (cycle_index - 1 - cycle_step) % cycle_size
        )

    total = lax.fori_loop(1, cycle_size, single_step, owner_term((cycle_index - 1) % cycle_size))
    summed = lax.psum(total, "dp")
    tokens_all = local_tokens * cycle_size * lax.axis_size("dp")
    grad_weight = summed * (1.0 / math.sqrt(tokens_all))
    return (grad_inputs, grad_weight)


def solution(mesh):
    in_specs = (
        P(("blk", "dp"), None),
        P(("blk", "dp"), None),
        P(("blk", "dp"), None),
        P(("blk", "dp"), None),
        P(("blk", "dp"), None),
        P("blk", None),
    )
    out_specs = (P(("blk", "dp"), None), P("blk", None))
    return jax.shard_map(local, mesh=mesh, in_specs=in_specs, out_specs=out_specs, check_vma=False)
```

profile of v0, /device:TPU:0, one launch (start us, length us, event | category | flops | bytes accessed | tf_op | source)
XLA Modules:
  0.0 213.0 jit_solution(4162167666595354681)
XLA Ops:
  8.0 0.0 copy-start.2
  8.0 0.0 all-reduce.2.cloned.1.call-start
  8.1 1.4 reshape.19
  9.5 0.8 broadcast_compare_fusion
  10.3 0.0 copy-done.2
  10.4 0.5 fusion.21
  10.9 0.0 copy-start.1
  10.9 0.3 fusion.6
  11.2 0.7 copy-done.1
  11.9 0.3 copy.18
  12.2 0.4 fusion.7
  12.6 0.1 copy.12
  12.8 1.3 fusion.11
  14.1 126.0 %while.15 = (s32[]{:T(128)}, f32[288,1024]{1,0:T(8,128)S(1)}, s32[]{:T(128)}, bf16[128,2304]{1,0:T(8,128)(2,1)}, bf16[128,1024]{1,0:T(8,128)(2,1)S(1)}, /*index=...) while((s32[]{:T(128)}, f32[288,1024]{1,0:T(8,128)S(1)}, s32[]{:T(128)}, ...), condition=%wide.region_3.4_spmd, body=%wide.region_2.3_spmd.sunk | while | flops 75792400 | bytes 7438656 | solution.py:66
  14.2 0.5 collective-permute-start
  14.7 16.8 %collective-permute-done = f32[288,1024]{1,0:T(8,128)S(1)} collective-permute-done((f32[288,1024]{1,0:T(8,128)S(1)}, f32[288,1024]{1,0:T(8,128)S(1)}, u32[]{:S(2)}, u32[]{:S(2)}) %collective-permute-start) | collective-permute-done | bytes 1179680 | tf_op jit(solution)/shard_map/while/body/eval_jaxpr/ppermute | solution.py:19
  31.4 1.3 convolution_add_fusion.2
  32.8 0.1 collective-permute-start
  32.9 16.5 %collective-permute-done = f32[288,1024]{1,0:T(8,128)S(1)} collective-permute-done((f32[288,1024]{1,0:T(8,128)S(1)}, f32[288,1024]{1,0:T(8,128)S(1)}, u32[]{:S(2)}, u32[]{:S(2)}) %collective-permute-start) | collective-permute-done | bytes 1179680 | tf_op jit(solution)/shard_map/while/body/eval_jaxpr/ppermute | solution.py:19
  49.3 1.3 convolution_add_fusion.2
  50.7 0.1 collective-permute-start
  50.8 16.5 %collective-permute-done = f32[288,1024]{1,0:T(8,128)S(1)} collective-permute-done((f32[288,1024]{1,0:T(8,128)S(1)}, f32[288,1024]{1,0:T(8,128)S(1)}, u32[]{:S(2)}, u32[]{:S(2)}) %collective-permute-start) | collective-permute-done | bytes 1179680 | tf_op jit(solution)/shard_map/while/body/eval_jaxpr/ppermute | solution.py:19
  67.2 1.3 convolution_add_fusion.2
  68.6 0.1 collective-permute-start
  68.7 16.5 %collective-permute-done = f32[288,1024]{1,0:T(8,128)S(1)} collective-permute-done((f32[288,1024]{1,0:T(8,128)S(1)}, f32[288,1024]{1,0:T(8,128)S(1)}, u32[]{:S(2)}, u32[]{:S(2)}) %collective-permute-start) | collective-permute-done | bytes 1179680 | tf_op jit(solution)/shard_map/while/body/eval_jaxpr/ppermute | solution.py:19
  85.1 1.3 convolution_add_fusion.2
  86.5 0.1 collective-permute-start
  86.6 16.5 %collective-permute-done = f32[288,1024]{1,0:T(8,128)S(1)} collective-permute-done((f32[288,1024]{1,0:T(8,128)S(1)}, f32[288,1024]{1,0:T(8,128)S(1)}, u32[]{:S(2)}, u32[]{:S(2)}) %collective-permute-start) | collective-permute-done | bytes 1179680 | tf_op jit(solution)/shard_map/while/body/eval_jaxpr/ppermute | solution.py:19
  103.1 1.3 convolution_add_fusion.2
  104.4 0.1 collective-permute-start
  104.5 16.5 %collective-permute-done = f32[288,1024]{1,0:T(8,128)S(1)} collective-permute-done((f32[288,1024]{1,0:T(8,128)S(1)}, f32[288,1024]{1,0:T(8,128)S(1)}, u32[]{:S(2)}, u32[]{:S(2)}) %collective-permute-start) | collective-permute-done | bytes 1179680 | tf_op jit(solution)/shard_map/while/body/eval_jaxpr/ppermute | solution.py:19
  121.0 1.3 convolution_add_fusion.2
  122.3 0.1 collective-permute-start
  122.4 16.5 %collective-permute-done = f32[288,1024]{1,0:T(8,128)S(1)} collective-permute-done((f32[288,1024]{1,0:T(8,128)S(1)}, f32[288,1024]{1,0:T(8,128)S(1)}, u32[]{:S(2)}, u32[]{:S(2)}) %collective-permute-start) | collective-permute-done | bytes 1179680 | tf_op jit(solution)/shard_map/while/body/eval_jaxpr/ppermute | solution.py:19
  138.9 1.3 convolution_add_fusion.2
  140.2 0.0 copy-start
  140.2 1.0 copy-done
  141.2 0.0 all-reduce.2.cloned.1.call-update
  141.2 0.0 all-gather.2.cloned.1.call-start
  141.3 0.5 all-gather.2.cloned.1.call-update
  141.8 56.5 %all-reduce.2.cloned.1.call-done = f32[288,1024]{1,0:T(8,128)} async-done(((f32[288,1024]{1,0:T(8,128)}), f32[288,1024]{1,0:T(8,128)}) %all-reduce.2.cloned.1.call-update) | async-done | bytes 1179664 | tf_op jit(solution)/shard_map/psum | solution.py:67
  198.3 2.4 %broadcast_multiply_fusion = f32[288,1024]{1,0:T(8,128)} fusion(f32[288,1024]{1,0:T(8,128)} %all-reduce.2.cloned.1.call-done), kind=kLoop, calls=%fused_computation.13 | loop fusion | flops 294912 | bytes 2359296 | tf_op jit(solution)/shard_map/mul | solution.py:69
  200.8 0.0 all-gather.2.cloned.1.call-done
  200.8 4.8 %convolution_convert_fusion = bf16[128,2304]{1,0:T(8,128)(2,1)} fusion(bf16[128,1024]{0,1:T(8,128)(2,1)S(1)} %bitcast.32, bf16[2304,1024]{1,0:T(8,128)(2,1)} %all-gather.2.cloned.1.call-done), kind=kOutput, calls=%fused_computation.4 | convolution fusion | flops 604274688 | bytes 5570560 | tf_op jit(solution)/shard_map/dot_general | solution.py:48
  (1 shorter events, 0.0 us)
Async XLA Ops:
  8.0 2.3 %copy-start.2 = (bf16[128,1024]{1,0:T(8,128)(2,1)S(1)}, bf16[128,1024]{1,0:T(8,128)(2,1)}, u32[]{:S(2)}) copy-start(bf16[128,1024]{1,0:T(8,128)(2,1)} %param.10) | copy-start | bytes 786436
  8.0 190.3 %all-reduce.2.cloned.1.call-start = ((), (), s32[]{:S(2)}) async-start(), calls=%async_computation.1 | async-start | bytes 2359296 | tf_op jit(solution)/shard_map/psum | solution.py:67
  10.9 1.0 copy-start.1
  14.2 17.3 %collective-permute-start = (f32[288,1024]{1,0:T(8,128)S(1)}, f32[288,1024]{1,0:T(8,128)S(1)}, u32[]{:S(2)}, u32[]{:S(2)}) collective-permute-start(f32[288,1024]{1,0:T(8,128)S(1)} %get-tuple-element.197), channel_id=1, source_target_pairs={{0,4},{4,8},{8,12},{12,16},{16,20},{20,24},{24,28},{28,0},{1,5},{5... | collective-permute-start | bytes 3538952 | tf_op jit(solution)/shard_map/while/body/eval_jaxpr/ppermute | solution.py:19
  32.8 16.6 %collective-permute-start = (f32[288,1024]{1,0:T(8,128)S(1)}, f32[288,1024]{1,0:T(8,128)S(1)}, u32[]{:S(2)}, u32[]{:S(2)}) collective-permute-start(f32[288,1024]{1,0:T(8,128)S(1)} %get-tuple-element.197), channel_id=1, source_target_pairs={{0,4},{4,8},{8,12},{12,16},{16,20},{20,24},{24,28},{28,0},{1,5},{5... | collective-permute-start | bytes 3538952 | tf_op jit(solution)/shard_map/while/body/eval_jaxpr/ppermute | solution.py:19
  50.7 16.6 %collective-permute-start = (f32[288,1024]{1,0:T(8,128)S(1)}, f32[288,1024]{1,0:T(8,128)S(1)}, u32[]{:S(2)}, u32[]{:S(2)}) collective-permute-start(f32[288,1024]{1,0:T(8,128)S(1)} %get-tuple-element.197), channel_id=1, source_target_pairs={{0,4},{4,8},{8,12},{12,16},{16,20},{20,24},{24,28},{28,0},{1,5},{5... | collective-permute-start | bytes 3538952 | tf_op jit(solution)/shard_map/while/body/eval_jaxpr/ppermute | solution.py:19
  68.6 16.6 %collective-permute-start = (f32[288,1024]{1,0:T(8,128)S(1)}, f32[288,1024]{1,0:T(8,128)S(1)}, u32[]{:S(2)}, u32[]{:S(2)}) collective-permute-start(f32[288,1024]{1,0:T(8,128)S(1)} %get-tuple-element.197), channel_id=1, source_target_pairs={{0,4},{4,8},{8,12},{12,16},{16,20},{20,24},{24,28},{28,0},{1,5},{5... | collective-permute-start | bytes 3538952 | tf_op jit(solution)/shard_map/while/body/eval_jaxpr/ppermute | solution.py:19
  86.5 16.6 %collective-permute-start = (f32[288,1024]{1,0:T(8,128)S(1)}, f32[288,1024]{1,0:T(8,128)S(1)}, u32[]{:S(2)}, u32[]{:S(2)}) collective-permute-start(f32[288,1024]{1,0:T(8,128)S(1)} %get-tuple-element.197), channel_id=1, source_target_pairs={{0,4},{4,8},{8,12},{12,16},{16,20},{20,24},{24,28},{28,0},{1,5},{5... | collective-permute-start | bytes 3538952 | tf_op jit(solution)/shard_map/while/body/eval_jaxpr/ppermute | solution.py:19
  104.4 16.6 %collective-permute-start = (f32[288,1024]{1,0:T(8,128)S(1)}, f32[288,1024]{1,0:T(8,128)S(1)}, u32[]{:S(2)}, u32[]{:S(2)}) collective-permute-start(f32[288,1024]{1,0:T(8,128)S(1)} %get-tuple-element.197), channel_id=1, source_target_pairs={{0,4},{4,8},{8,12},{12,16},{16,20},{20,24},{24,28},{28,0},{1,5},{5... | collective-permute-start | bytes 3538952 | tf_op jit(solution)/shard_map/while/body/eval_jaxpr/ppermute | solution.py:19
  122.3 16.6 %collective-permute-start = (f32[288,1024]{1,0:T(8,128)S(1)}, f32[288,1024]{1,0:T(8,128)S(1)}, u32[]{:S(2)}, u32[]{:S(2)}) collective-permute-start(f32[288,1024]{1,0:T(8,128)S(1)} %get-tuple-element.197), channel_id=1, source_target_pairs={{0,4},{4,8},{8,12},{12,16},{16,20},{20,24},{24,28},{28,0},{1,5},{5... | collective-permute-start | bytes 3538952 | tf_op jit(solution)/shard_map/while/body/eval_jaxpr/ppermute | solution.py:19
  140.2 1.0 copy-start
  141.2 59.5 %all-gather.2.cloned.1.call-start = ((), (), s32[]{:S(2)}) async-start(), calls=%async_computation | async-start | bytes 5308416 | tf_op jit(solution)/shard_map/all_gather | solution.py:50
Sparse Core Ops, SparseCore 0:
  141.3 56.9 all-reduce.1
Sparse Core Ops, SparseCore 1:
  143.6 39.8 all-gather.1
where the time goes:
time: 213 us
  waiting for transfers between devices  173 us (81%)
  matrix products  16.6 us (8%)
  between operations  15.6 us (7%)
  local copies, waits for them, and re-layouts  3.6 us (2%)
  other arithmetic  3.23 us (2%)
    ppermute x7, waiting for transfers between devices, from_behind(): return lax.ppermute(value, axis, pairs)  116 us
    psum x1, waiting for transfers between devices, local(): summed = lax.psum(total, 'dp')  56.5 us
    dot_general x8, matrix products, owner_term(): lax.dot_general(columns, value_grad, (((0,), (0,)), ((), ())), preferred_...  10.5 us
    dot_general x1, matrix products, local(): lax.dot_general(value_grad, lax.all_gather(value_weight, 'blk', axis=0, t...  4.85 us
  transfers between devices with their start and end apart: 9, of which 8 were waited for; matrix products, arithmetic and copies ran while one was open for 1% of the time, Pallas kernels for 0%

commit v1 on v0

--- a/solution.py
+++ b/solution.py
@@ -1,8 +1,11 @@
+import functools
 import math
 
 import jax
 import jax.numpy as jnp
 from jax import lax
+from jax.experimental import pallas as pl
+from jax.experimental.pallas import tpu as pltpu
 from jax.sharding import PartitionSpec as P
 
 KV_HEADS = 8
@@ -70,6 +73,258 @@
     return (grad_inputs, grad_weight)
 
 
+CHUNKS = 4
+DIRECT = (1, 2, 4, 6)
+CROSS = (2, 4, 6)
+MESH = pl.DeviceIdType.MESH
+
+
+def other(index, d):
+    core, x, y = index % 2, (index // 2) % 2, index // 4
+    core = 1 - core if d & 1 else core
+    x = 1 - x if d & 2 else x
+    y = 1 - y if d & 4 else y
+    return y * 4 + x * 2 + core
+
+
+def fused_kernel(
+    scale,
+    x_ref, q_ref, k_ref, g_ref, seg_ref, w_ref,
+    gi_ref, gw_ref,
+    xs, xr, vg, gis, gir, part, za, zb, zs, zt,
+    xs_sem, xr_sem, vs_sem, vr_sem, fs_sem, fr_sem, gs_sem, gr_sem,
+    z1s, z1r, z2s, z2r, z3s, z3r,
+):
+    tokens, features = x_ref.shape
+    rows, width = w_ref.shape
+    step = width // CHUNKS
+    heads_per_chunk = step // HEAD_DIM
+    i = lax.axis_index("blk")
+    z = lax.axis_index("dp")
+    z_pair = z + 1 - 2 * (z % 2)
+    z_across = 3 - z
+    edge = z % 3 == 0
+
+    barrier = pltpu.get_barrier_semaphore()
+    for d in range(1, 8):
+        pl.semaphore_signal(barrier, inc=1, device_id=(other(i, d), z), device_id_type=MESH)
+    pl.semaphore_signal(barrier, inc=1, device_id=(i, z_pair), device_id_type=MESH)
+    pl.semaphore_signal(barrier, inc=1, device_id=(i, z_across), device_id_type=MESH)
+
+    for b in range(features // 128):
+        xs[128 * b : 128 * (b + 1), :] = x_ref[:, 128 * b : 128 * (b + 1)].T
+    pl.semaphore_wait(barrier, 9)
+
+    def my_rows(index):
+        return pl.ds(pl.multiple_of(index * rows, 32), rows)
+
+    def x_copy(d):
+        peer = other(i, d)
+        return pltpu.make_async_remote_copy(
+            src_ref=xs.at[my_rows(peer), :],
+            dst_ref=xr.at[:, pl.ds(tokens * d, tokens)],
+            send_sem=xs_sem.at[d], recv_sem=xr_sem.at[d],
+            device_id=(peer, z), device_id_type=MESH,
+        )
+
+    def v_copy(k, n):
+        d = DIRECT[n]
+        columns = pl.ds(step * k, step)
+        return pltpu.make_async_remote_copy(
+            src_ref=vg.at[pl.ds(0, tokens), columns],
+            dst_ref=vg.at[pl.ds(tokens * d, tokens), columns],
+            send_sem=vs_sem.at[k, n], recv_sem=vr_sem.at[k, n],
+            device_id=(other(i, d), z), device_id_type=MESH,
+        )
+
+    def f_copy(k, n):
+        d = CROSS[n]
+        columns = pl.ds(step * k, step)
+        return pltpu.make_async_remote_copy(
+            src_ref=vg.at[pl.ds(tokens * d, tokens), columns],
+            dst_ref=vg.at[pl.ds(tokens * (d + 1), tokens), columns],
+            send_sem=fs_sem.at[k, n], recv_sem=fr_sem.at[k, n],
+            device_id=(other(i, 1), z), device_id_type=MESH,
+        )
+
+    def g_copy(d):
+        return pltpu.make_async_remote_copy(
+            src_ref=gis.at[:, pl.ds(tokens * d, tokens)],
+            dst_ref=gir.at[my_rows(i), :],
+            send_sem=gs_sem.at[d], recv_sem=gr_sem.at[d],
+            device_id=(other(i, d), z), device_id_type=MESH,
+        )
+
+    def z_copy(src, dst, send, recv, k, target):
+        return pltpu.make_async_remote_copy(
+            src_ref=src.at[k], dst_ref=dst.at[k], send_sem=send.at[k], recv_sem=recv.at[k],
+            device_id=(i, target), device_id_type=MESH,
+        )
+
+    def z_first(k):
+        return z_copy(zs, za, z1s, z1r, k, z_pair)
+
+    def z_second(k):
+        return z_copy(zs, zb, z2s, z2r, k, z_across)
+
+    def z_third(k):
+        return z_copy(zt, za, z3s, z3r, k, z_pair)
+
+    for d in (6, 7, 2, 3, 4, 5, 1):
+        x_copy(d).start()
+    xr[:, 0:tokens] = xs[my_rows(i), :]
+
+    seg_row = jnp.broadcast_to(seg_ref[...].astype(jnp.float32), (tokens, tokens))
+    allowed = seg_row.T <= seg_row
+    allowed = jnp.concatenate([allowed.astype(jnp.float32)] * GROUP, axis=1) > 0.5
+    for j in range(KV_HEADS):
+        base = GROUP * HEAD_DIM * j
+        heads = [slice(base + HEAD_DIM * h, base + HEAD_DIM * (h + 1)) for h in range(GROUP)]
+        q2 = jnp.concatenate([q_ref[:, h] for h in heads], axis=0)
+        g2 = jnp.concatenate([g_ref[:, h] for h in heads], axis=0)
+        own = slice(HEAD_DIM * j, HEAD_DIM * (j + 1))
+        scores = query_scale * lax.dot_general(
+            k_ref[:, own], q2, (((1,), (1,)), ((), ())), preferred_element_type=jnp.float32
+        )
+        scores = jnp.where(allowed, scores, -jnp.inf)
+        weights = jnp.exp(scores - jnp.max(scores, axis=0, keepdims=True))
+        probs = (weights / jnp.sum(weights, axis=0, keepdims=True)).astype(jnp.bfloat16)
+        vg[0:tokens, own] = jnp.dot(probs, g2, preferred_element_type=jnp.float32).astype(jnp.bfloat16)
+        if (j + 1) % heads_per_chunk == 0:
+            for n in (3, 1, 2, 0):
+                v_copy(j // heads_per_chunk, n).start()
+
+    def second(k):
+        @pl.when(jnp.logical_not(edge))
+        def _():
+            z_first(k).wait_recv()
+            zs[k] = (part[k] + za[k].astype(jnp.float32)).astype(jnp.bfloat16)
+            z_second(k).start()
+
+    def third(k):
+        @pl.when(jnp.logical_not(edge))
+        def _():
+            z_second(k).wait_recv()
+            total = (zs[k].astype(jnp.float32) + zb[k].astype(jnp.float32)).astype(jnp.bfloat16)
+            zt[k] = total
+            z_third(k).start()
+            gw_ref[:, step * k : step * (k + 1)] = total.astype(jnp.float32) * scale
+
+    for k in range(CHUNKS):
+        for n in range(3):
+            v_copy(k, n + 1).wait_recv()
+            f_copy(k, n).start()
+        if k == 0:
+            for d in range(1, 8):
+                x_copy(d).wait_recv()
+        v_copy(k, 0).wait_recv()
+        for n in range(3):
+            f_copy(k, n).wait_recv()
+        part[k] = jnp.dot(
+            xr[...], vg[:, step * k : step * (k + 1)], preferred_element_type=jnp.float32
+        )
+
+        @pl.when(edge)
+        def _():
+            zs[k] = part[k].astype(jnp.bfloat16)
+            z_first(k).start()
+
+        if k >= 1:
+            second(k - 1)
+        if k >= 2:
+            third(k - 2)
+
+    gis[...] = lax.dot_general(
+        w_ref[...], vg[...], (((1,), (1,)), ((), ())), preferred_element_type=jnp.float32
+    ).astype(jnp.bfloat16)
+    for d in (6, 7, 2, 3, 4, 5, 1):
+        g_copy(d).start()
+    gir[my_rows(i), :] = gis[:, 0:tokens]
+    second(CHUNKS - 1)
+    third(CHUNKS - 2)
+    third(CHUNKS - 1)
+
+    for d in range(1, 8):
+        pltpu.make_async_remote_copy(
+            src_ref=gis.at[:, pl.ds(tokens * d, tokens)],
+            dst_ref=gir.at[my_rows(other(i, d)), :],
+            send_sem=gs_sem.at[d], recv_sem=gr_sem.at[d],
+            device_id=(other(i, d), z), device_id_type=MESH,
+        ).wait_recv()
+    for b in range(features // 128):
+        gi_ref[:, 128 * b : 128 * (b + 1)] = gir[128 * b : 128 * (b + 1), :].T
+
+    @pl.when(edge)
+    def _():
+        for k in range(CHUNKS):
+            z_third(k).wait_recv()
+            gw_ref[:, step * k : step * (k + 1)] = za[k].astype(jnp.float32) * scale
+            z_first(k).wait_send()
+
+    @pl.when(jnp.logical_not(edge))
+    def _():
+        for k in range(CHUNKS):
+            z_second(k).wait_send()
+            z_third(k).wait_send()
+
+    for d in range(1, 8):
+        x_copy(d).wait_send()
+        g_copy(d).wait_send()
+    for k in range(CHUNKS):
+        for n in range(4):
+            v_copy(k, n).wait_send()
+        for n in range(3):
+            f_copy(k, n).wait_send()
+
+
+def fused(inputs, queries, keys, grad_attn, segment_ids, value_weight):
+    tokens, features = inputs.shape
+    rows, width = value_weight.shape
+    blocks = lax.axis_size("blk")
+    tokens_all = tokens * blocks * lax.axis_size("dp")
+    step = width // CHUNKS
+    dma = pltpu.SemaphoreType.DMA
+    bf16 = jnp.bfloat16
+    chunked = pltpu.VMEM((CHUNKS, rows, step), bf16)
+    return pl.pallas_call(
+        functools.partial(fused_kernel, 1.0 / math.sqrt(tokens_all)),
+        out_shape=(
+            jax.ShapeDtypeStruct((tokens, features), bf16),
+            jax.ShapeDtypeStruct((rows, width), jnp.float32),
+        ),
+        in_specs=[pl.BlockSpec(memory_space=pltpu.VMEM)] * 6,
+        out_specs=(pl.BlockSpec(memory_space=pltpu.VMEM),) * 2,
+        scratch_shapes=[
+            pltpu.VMEM((features, tokens), bf16),
+            pltpu.VMEM((rows, blocks * tokens), bf16),
+            pltpu.VMEM((blocks * tokens, width), bf16),
+            pltpu.VMEM((rows, blocks * tokens), bf16),
+            pltpu.VMEM((features, tokens), bf16),
+            pltpu.VMEM((CHUNKS, rows, step), jnp.float32),
+            chunked, chunked, chunked, chunked,
+            dma((8,)), dma((8,)),
+            dma((CHUNKS, 4)), dma((CHUNKS, 4)),
+            dma((CHUNKS, 3)), dma((CHUNKS, 3)),
+            dma((8,)), dma((8,)),
+            dma((CHUNKS,)), dma((CHUNKS,)), dma((CHUNKS,)), dma((CHUNKS,)), dma((CHUNKS,)), dma((CHUNKS,)),
+        ],
+        compiler_params=pltpu.CompilerParams(
+            collective_id=0, has_side_effects=True, vmem_limit_bytes=40 * 1024 * 1024
+        ),
+    )(inputs, queries, keys, grad_attn, segment_ids, value_weight)
+
+
+def plan(inputs, queries, keys, grad_attn, segment_ids, value_weight):
+    fits = (
+        lax.axis_size("blk") == 8
+        and lax.axis_size("dp") == 4
+        and inputs.shape[0] == HEAD_DIM
+        and value_weight.shape[0] % 32 == 0
+    )
+    chosen = fused if fits else local
+    return chosen(inputs, queries, keys, grad_attn, segment_ids, value_weight)
+
+
 def solution(mesh):
     in_specs = (
         P(("blk", "dp"), None),
@@ -80,4 +335,4 @@
         P("blk", None),
     )
     out_specs = (P(("blk", "dp"), None), P("blk", None))
-    return jax.shard_map(local, mesh=mesh, in_specs=in_specs, out_specs=out_specs, check_vma=False)
+    return jax.shard_map(plan, mesh=mesh, in_specs=in_specs, out_specs=out_specs, check_vma=False)

time: 213 us -> 53.7 us (0.25)
  waiting for transfers between devices: 173 us -> 0 us
  Pallas kernels: 0 us -> 45 us
  matrix products: 16.6 us -> 0 us
  between operations: 15.6 us -> 0.65 us
  local copies, waits for them, and re-layouts: 3.6 us -> 7.64 us
  other arithmetic: 3.23 us -> 0 us
    ppermute x7 -> x0, waiting for transfers between devices: 116 us -> none  [from_behind(): return lax.ppermute(value, axis, pairs)]
    psum x1 -> x0, waiting for transfers between devices: 56.5 us -> none  [local(): summed = lax.psum(total, 'dp')]
    pallas_call x0 -> x1, Pallas kernels: none -> 45 us  [fused(): pl.pallas_call(functools.partial(fused_kernel, 1.0 / math.sqrt(tokens_all...]
    dot_general x11 -> x0, matrix products: 16.1 us -> none  [the longest x8 10.5 us: owner_term(): lax.dot_general(columns, value_grad, (((0,), (0,)), ((), ())), preferred_...]
    unnamed x7 -> x14, local copies, waits for them, and re-layouts: 1.75 us -> 7.64 us
    mul x1 -> x0, other arithmetic: 2.42 us -> none  [local(): grad_weight = summed * (1.0 / math.sqrt(tokens_all))]
  transfers between devices with their start and end apart: 9 -> 0, of which waited for: 8 -> 0; matrix products, arithmetic and copies ran while one was open for 1% -> 0% of each run, Pallas kernels for 0% -> 0%
where the time goes in v1:
time: 53.7 us; the launch traced here: 53.3 us
  Pallas kernels  45 us (84%)
  local copies, waits for them, and re-layouts  7.64 us (14%)
  between operations  0.65 us (1%)
    pallas_call x1, Pallas kernels, fused(): pl.pallas_call(functools.partial(fused_kernel, 1.0 / math.sqrt(tokens_all...  45 us
    unnamed x14, local copies, waits for them, and re-layouts  7.64 us

profile of v1, /device:TPU:0, one launch (start us, length us, event | category | flops | bytes accessed | tf_op | source)
XLA Modules:
  0.0 53.3 jit_solution(8630827276667960775)
XLA Ops:
  0.6 0.0 copy-start
  0.6 1.1 %copy-done = bf16[128,2304]{1,0:T(8,128)(2,1)S(1)} copy-done((bf16[128,2304]{1,0:T(8,128)(2,1)S(1)}, bf16[128,2304]{1,0:T(8,128)(2,1)}, u32[]{:S(2)}) %copy-start) | copy-done | bytes 589848
  1.7 0.0 copy-start.1
  1.7 1.1 %copy-done.1 = bf16[288,1024]{1,0:T(8,128)(2,1)S(1)} copy-done((bf16[288,1024]{1,0:T(8,128)(2,1)S(1)}, bf16[288,1024]{1,0:T(8,128)(2,1)}, u32[]{:S(2)}) %copy-start.1) | copy-done | bytes 589848
  2.8 0.0 copy-start.2
  2.8 1.0 %copy-done.2 = bf16[128,2048]{1,0:T(8,128)(2,1)S(1)} copy-done((bf16[128,2048]{1,0:T(8,128)(2,1)S(1)}, bf16[128,2048]{1,0:T(8,128)(2,1)}, u32[]{:S(2)}) %copy-start.2) | copy-done | bytes 524312
  3.8 0.0 copy-start.3
  3.8 1.0 %copy-done.3 = bf16[128,2048]{1,0:T(8,128)(2,1)S(1)} copy-done((bf16[128,2048]{1,0:T(8,128)(2,1)S(1)}, bf16[128,2048]{1,0:T(8,128)(2,1)}, u32[]{:S(2)}) %copy-start.3) | copy-done | bytes 524312
  4.8 0.0 copy-start.4
  4.8 0.9 %copy-done.4 = bf16[128,1024]{1,0:T(8,128)(2,1)S(1)} copy-done((bf16[128,1024]{1,0:T(8,128)(2,1)S(1)}, bf16[128,1024]{1,0:T(8,128)(2,1)}, u32[]{:S(2)}) %copy-start.4) | copy-done | bytes 262168
  5.8 0.0 copy-start.5
  5.8 0.7 %copy-done.5 = s32[1,128]{1,0:T(1,128)S(1)} copy-done((s32[1,128]{1,0:T(1,128)S(1)}, s32[1,128]{1,0:T(1,128)}, u32[]{:S(2)}) %copy-start.5) | copy-done | bytes 536
  6.5 45.0 %shard_map.77 = (bf16[128,2304]{1,0:T(8,128)(2,1)S(1)}, f32[288,1024]{1,0:T(8,128)S(1)}) custom-call(bf16[128,2304]{1,0:T(8,128)(2,1)S(1)} %copy-done, bf16[128,2048]{1,0:T(8,128)(2,1)S(1)} %copy-done.2, bf16[128,1024]{1,0:T(8,128)(2,1)S(1)} %copy-done.4, bf16[128,2048]{1,0:T(8,128)(2,1)S(1)} %copy-done.3, s32[1,128]{1,0:T(1,128)S(1)} %copy-done.5, ...), custom_call_target="tpu_custom_call" | custom-call | tf_op jit(solution)/shard_map/pallas_call | solution.py:289
  51.5 0.8 %copy.10 = bf16[128,2304]{1,0:T(8,128)(2,1)} copy(bf16[128,2304]{1,0:T(8,128)(2,1)S(1)} %get-tuple-element.4) | data formatting | bytes 1179648
  52.3 1.0 %copy.11 = f32[288,1024]{1,0:T(8,128)} copy(f32[288,1024]{1,0:T(8,128)S(1)} %get-tuple-element.5) | data formatting | bytes 2359296
Async XLA Ops:
  0.6 1.1 %copy-start = (bf16[128,2304]{1,0:T(8,128)(2,1)S(1)}, bf16[128,2304]{1,0:T(8,128)(2,1)}, u32[]{:S(2)}) copy-start(bf16[128,2304]{1,0:T(8,128)(2,1)} %x_ref.1) | copy-start | bytes 1769476
  1.7 1.1 %copy-start.1 = (bf16[288,1024]{1,0:T(8,128)(2,1)S(1)}, bf16[288,1024]{1,0:T(8,128)(2,1)}, u32[]{:S(2)}) copy-start(bf16[288,1024]{1,0:T(8,128)(2,1)} %w_ref.1) | copy-start | bytes 1769476
  2.8 1.0 %copy-start.2 = (bf16[128,2048]{1,0:T(8,128)(2,1)S(1)}, bf16[128,2048]{1,0:T(8,128)(2,1)}, u32[]{:S(2)}) copy-start(bf16[128,2048]{1,0:T(8,128)(2,1)} %q_ref.1) | copy-start | bytes 1572868
  3.8 1.0 %copy-start.3 = (bf16[128,2048]{1,0:T(8,128)(2,1)S(1)}, bf16[128,2048]{1,0:T(8,128)(2,1)}, u32[]{:S(2)}) copy-start(bf16[128,2048]{1,0:T(8,128)(2,1)} %g_ref.1) | copy-start | bytes 1572868
  4.8 0.9 %copy-start.4 = (bf16[128,1024]{1,0:T(8,128)(2,1)S(1)}, bf16[128,1024]{1,0:T(8,128)(2,1)}, u32[]{:S(2)}) copy-start(bf16[128,1024]{1,0:T(8,128)(2,1)} %k_ref.1) | copy-start | bytes 786436
  5.8 0.7 %copy-start.5 = (s32[1,128]{1,0:T(1,128)S(1)}, s32[1,128]{1,0:T(1,128)}, u32[]{:S(2)}) copy-start(s32[1,128]{1,0:T(1,128)} %seg_ref.1) | copy-start | bytes 1540

commit v2 on v1

--- a/solution.py
+++ b/solution.py
@@ -74,6 +74,8 @@
 
 
 CHUNKS = 4
+SPLIT = 3
+PAIRS = (6, 2, 4, 0)
 DIRECT = (1, 2, 4, 6)
 CROSS = (2, 4, 6)
 MESH = pl.DeviceIdType.MESH
@@ -89,9 +91,10 @@
 
 def fused_kernel(
     scale,
-    x_ref, q_ref, k_ref, g_ref, seg_ref, w_ref,
+    x_hbm, q_hbm, k_hbm, g_hbm, seg_hbm, w_hbm,
     gi_ref, gw_ref,
-    xs, xr, vg, gis, gir, part, za, zb, zs, zt,
+    x_ref, q_ref, k_ref, g_ref, seg_ref, w_ref, in_sem,
+    xs, xr, vg, gis, gir, part, gacc, za, zb, zs, zt,
     xs_sem, xr_sem, vs_sem, vr_sem, fs_sem, fr_sem, gs_sem, gr_sem,
     z1s, z1r, z2s, z2r, z3s, z3r,
 ):
@@ -105,12 +108,24 @@
     z_across = 3 - z
     edge = z % 3 == 0
 
+    loads = [
+        pltpu.make_async_copy(src, dst, in_sem.at[n])
+        for n, (src, dst) in enumerate(
+            (
+                (x_hbm, x_ref), (seg_hbm, seg_ref), (k_hbm, k_ref),
+                (q_hbm, q_ref), (g_hbm, g_ref), (w_hbm, w_ref),
+            )
+        )
+    ]
+    for load in loads:
+        load.start()
     barrier = pltpu.get_barrier_semaphore()
     for d in range(1, 8):
         pl.semaphore_signal(barrier, inc=1, device_id=(other(i, d), z), device_id_type=MESH)
     pl.semaphore_signal(barrier, inc=1, device_id=(i, z_pair), device_id_type=MESH)
     pl.semaphore_signal(barrier, inc=1, device_id=(i, z_across), device_id_type=MESH)
 
+    loads[0].wait()
     for b in range(features // 128):
         xs[128 * b : 128 * (b + 1), :] = x_ref[:, 128 * b : 128 * (b + 1)].T
     pl.semaphore_wait(barrier, 9)
@@ -155,6 +170,14 @@
             device_id=(other(i, d), z), device_id_type=MESH,
         )
 
+    def g_arrival(d):
+        return pltpu.make_async_remote_copy(
+            src_ref=gis.at[:, pl.ds(tokens * d, tokens)],
+            dst_ref=gir.at[my_rows(other(i, d)), :],
+            send_sem=gs_sem.at[d], recv_sem=gr_sem.at[d],
+            device_id=(other(i, d), z), device_id_type=MESH,
+        )
+
     def z_copy(src, dst, send, recv, k, target):
         return pltpu.make_async_remote_copy(
             src_ref=src.at[k], dst_ref=dst.at[k], send_sem=send.at[k], recv_sem=recv.at[k],
@@ -174,6 +197,8 @@
         x_copy(d).start()
     xr[:, 0:tokens] = xs[my_rows(i), :]
 
+    for load in loads[1:5]:
+        load.wait()
     seg_row = jnp.broadcast_to(seg_ref[...].astype(jnp.float32), (tokens, tokens))
     allowed = seg_row.T <= seg_row
     allowed = jnp.concatenate([allowed.astype(jnp.float32)] * GROUP, axis=1) > 0.5
@@ -194,23 +219,32 @@
             for n in (3, 1, 2, 0):
                 v_copy(j // heads_per_chunk, n).start()
 
+    height = rows // SPLIT
+
+    def pieces_of(k):
+        return [(SPLIT * k + h, slice(height * h, height * (h + 1))) for h in range(SPLIT)]
+
     def second(k):
         @pl.when(jnp.logical_not(edge))
         def _():
-            z_first(k).wait_recv()
-            zs[k] = (part[k] + za[k].astype(jnp.float32)).astype(jnp.bfloat16)
-            z_second(k).start()
+            for m, band in pieces_of(k):
+                z_first(m).wait_recv()
+                zs[m] = (part[k, band, :] + za[m].astype(jnp.float32)).astype(jnp.bfloat16)
+                z_second(m).start()
 
     def third(k):
         @pl.when(jnp.logical_not(edge))
         def _():
-            z_second(k).wait_recv()
-            total = (zs[k].astype(jnp.float32) + zb[k].astype(jnp.float32)).astype(jnp.bfloat16)
-            zt[k] = total
-            z_third(k).start()
-            gw_ref[:, step * k : step * (k + 1)] = total.astype(jnp.float32) * scale
-
+            for m, band in pieces_of(k):
+                z_second(m).wait_recv()
+                total = (zs[m].astype(jnp.float32) + zb[m].astype(jnp.float32)).astype(jnp.bfloat16)
+                zt[m] = total
+                z_third(m).start()
+                gw_ref[band, step * k : step * (k + 1)] = total.astype(jnp.float32) * scale
+
+    loads[5].wait()
     for k in range(CHUNKS):
+        columns = slice(step * k, step * (k + 1))
         for n in range(3):
             v_copy(k, n + 1).wait_recv()
             f_copy(k, n).start()
@@ -220,52 +254,57 @@
         v_copy(k, 0).wait_recv()
         for n in range(3):
             f_copy(k, n).wait_recv()
-        part[k] = jnp.dot(
-            xr[...], vg[:, step * k : step * (k + 1)], preferred_element_type=jnp.float32
-        )
+        part[k] = jnp.dot(xr[...], vg[:, columns], preferred_element_type=jnp.float32)
 
         @pl.when(edge)
         def _():
-            zs[k] = part[k].astype(jnp.bfloat16)
-            z_first(k).start()
-
+            for m, band in pieces_of(k):
+                zs[m] = part[k, band, :].astype(jnp.bfloat16)
+                z_first(m).start()
+
+        for d in PAIRS:
+            two = slice(tokens * d, tokens * (d + 2))
+            term = lax.dot_general(
+                w_ref[:, columns], vg[two, columns], (((1,), (1,)), ((), ())),
+                preferred_element_type=jnp.float32,
+            )
+            if k > 0:
+                term = gacc[:, two] + term
+            if k < CHUNKS - 1:
+                gacc[:, two] = term
+            else:
+                gis[:, two] = term.astype(jnp.bfloat16)
+                if d:
+                    g_copy(d).start()
+                g_copy(d + 1).start()
         if k >= 1:
             second(k - 1)
         if k >= 2:
             third(k - 2)
 
-    gis[...] = lax.dot_general(
-        w_ref[...], vg[...], (((1,), (1,)), ((), ())), preferred_element_type=jnp.float32
-    ).astype(jnp.bfloat16)
-    for d in (6, 7, 2, 3, 4, 5, 1):
-        g_copy(d).start()
     gir[my_rows(i), :] = gis[:, 0:tokens]
     second(CHUNKS - 1)
     third(CHUNKS - 2)
     third(CHUNKS - 1)
 
     for d in range(1, 8):
-        pltpu.make_async_remote_copy(
-            src_ref=gis.at[:, pl.ds(tokens * d, tokens)],
-            dst_ref=gir.at[my_rows(other(i, d)), :],
-            send_sem=gs_sem.at[d], recv_sem=gr_sem.at[d],
-            device_id=(other(i, d), z), device_id_type=MESH,
-        ).wait_recv()
+        g_arrival(d).wait_recv()
     for b in range(features // 128):
         gi_ref[:, 128 * b : 128 * (b + 1)] = gir[128 * b : 128 * (b + 1), :].T
 
     @pl.when(edge)
     def _():
         for k in range(CHUNKS):
-            z_third(k).wait_recv()
-            gw_ref[:, step * k : step * (k + 1)] = za[k].astype(jnp.float32) * scale
-            z_first(k).wait_send()
+            for m, band in pieces_of(k):
+                z_third(m).wait_recv()
+                gw_ref[band, step * k : step * (k + 1)] = za[m].astype(jnp.float32) * scale
+                z_first(m).wait_send()
 
     @pl.when(jnp.logical_not(edge))
     def _():
-        for k in range(CHUNKS):
-            z_second(k).wait_send()
-            z_third(k).wait_send()
+        for m in range(CHUNKS * SPLIT):
+            z_second(m).wait_send()
+            z_third(m).wait_send()
 
     for d in range(1, 8):
         x_copy(d).wait_send()
@@ -285,31 +324,38 @@
     step = width // CHUNKS
     dma = pltpu.SemaphoreType.DMA
     bf16 = jnp.bfloat16
-    chunked = pltpu.VMEM((CHUNKS, rows, step), bf16)
+    pieces = CHUNKS * SPLIT
+    chunked = pltpu.VMEM((pieces, rows // SPLIT, step), bf16)
     return pl.pallas_call(
         functools.partial(fused_kernel, 1.0 / math.sqrt(tokens_all)),
         out_shape=(
             jax.ShapeDtypeStruct((tokens, features), bf16),
             jax.ShapeDtypeStruct((rows, width), jnp.float32),
         ),
-        in_specs=[pl.BlockSpec(memory_space=pltpu.VMEM)] * 6,
+        in_specs=[pl.BlockSpec(memory_space=pl.ANY)] * 6,
         out_specs=(pl.BlockSpec(memory_space=pltpu.VMEM),) * 2,
         scratch_shapes=[
+            *(
+                pltpu.VMEM(operand.shape, operand.dtype)
+                for operand in (inputs, queries, keys, grad_attn, segment_ids, value_weight)
+            ),
+            dma((6,)),
             pltpu.VMEM((features, tokens), bf16),
             pltpu.VMEM((rows, blocks * tokens), bf16),
             pltpu.VMEM((blocks * tokens, width), bf16),
             pltpu.VMEM((rows, blocks * tokens), bf16),
             pltpu.VMEM((features, tokens), bf16),
             pltpu.VMEM((CHUNKS, rows, step), jnp.float32),
+            pltpu.VMEM((rows, blocks * tokens), jnp.float32),
             chunked, chunked, chunked, chunked,
             dma((8,)), dma((8,)),
             dma((CHUNKS, 4)), dma((CHUNKS, 4)),
             dma((CHUNKS, 3)), dma((CHUNKS, 3)),
             dma((8,)), dma((8,)),
-            dma((CHUNKS,)), dma((CHUNKS,)), dma((CHUNKS,)), dma((CHUNKS,)), dma((CHUNKS,)), dma((CHUNKS,)),
+            *([dma((pieces,))] * 6),
         ],
         compiler_params=pltpu.CompilerParams(
-            collective_id=0, has_side_effects=True, vmem_limit_bytes=40 * 1024 * 1024
+            collective_id=0, has_side_effects=True, vmem_limit_bytes=56 * 1024 * 1024
         ),
     )(inputs, queries, keys, grad_attn, segment_ids, value_weight)
 
@@ -320,6 +366,7 @@
         and lax.axis_size("dp") == 4
         and inputs.shape[0] == HEAD_DIM
         and value_weight.shape[0] % 32 == 0
+        and value_weight.shape[0] % (16 * SPLIT) == 0
     )
     chosen = fused if fits else local
     return chosen(inputs, queries, keys, grad_attn, segment_ids, value_weight)

time: 53.7 us -> 48.9 us (0.911)
  local copies, waits for them, and re-layouts: 7.64 us -> 3.03 us
    unnamed x14 -> x4, local copies, waits for them, and re-layouts: 7.64 us -> 3.03 us
where the time goes in v2:
time: 48.9 us; the launch traced here: 48.7 us
  Pallas kernels  45 us (92%)
  local copies, waits for them, and re-layouts  3.03 us (6%)
  between operations  0.65 us (1%)
    pallas_call x1, Pallas kernels, fused(): pl.pallas_call(functools.partial(fused_kernel, 1.0 / math.sqrt(tokens_all...  45 us
    unnamed x4, local copies, waits for them, and re-layouts  3.03 us

profile of v2, /device:TPU:0, one launch (start us, length us, event | category | flops | bytes accessed | tf_op | source)
XLA Modules:
  0.0 48.7 jit_solution(4802176244900627058)
XLA Ops:
  0.6 45.0 %shard_map.77 = (bf16[128,2304]{1,0:T(8,128)(2,1)}, f32[288,1024]{1,0:T(8,128)}) custom-call(bf16[128,2304]{1,0:T(8,128)(2,1)} %x_hbm.1, bf16[128,2048]{1,0:T(8,128)(2,1)} %q_hbm.1, bf16[128,1024]{1,0:T(8,128)(2,1)} %k_hbm.1, bf16[128,2048]{1,0:T(8,128)(2,1)} %g_hbm.1, s32[1,128]{1,0:T(1,128)} %seg_hbm.1, bf16[288,1024]{1,0:T(8,128)(2,1)} %w_hbm.1), custom_call_target="tpu_custom_call" | custom-call | tf_op jit(solution)/shard_map/pallas_call | solution.py:329
  45.7 0.0 copy-start
  45.7 2.0 %copy.10 = bf16[128,2304]{1,0:T(8,128)(2,1)} copy(bf16[128,2304]{1,0:T(8,128)(2,1)} %get-tuple-element.4) | data formatting | bytes 1179648
  47.7 0.0 copy-done
  47.7 1.0 %copy.11 = f32[288,1024]{1,0:T(8,128)} copy(f32[288,1024]{1,0:T(8,128)S(1)} %copy-done) | data formatting | bytes 2359296
Async XLA Ops:
  45.7 2.0 %copy-start = (f32[288,1024]{1,0:T(8,128)S(1)}, f32[288,1024]{1,0:T(8,128)}, u32[]{:S(2)}) copy-start(f32[288,1024]{1,0:T(8,128)} %get-tuple-element.5) | copy-start | bytes 3538948

commit v3 on v2

--- a/solution.py
+++ b/solution.py
@@ -90,7 +90,6 @@
 
 
 def fused_kernel(
-    scale,
     x_hbm, q_hbm, k_hbm, g_hbm, seg_hbm, w_hbm,
     gi_ref, gw_ref,
     x_ref, q_ref, k_ref, g_ref, seg_ref, w_ref, in_sem,
@@ -199,6 +198,10 @@
 
     for load in loads[1:5]:
         load.wait()
+    def start_chunk(k):
+        for n in (3, 1, 2, 0):
+            v_copy(k, n).start()
+
     seg_row = jnp.broadcast_to(seg_ref[...].astype(jnp.float32), (tokens, tokens))
     allowed = seg_row.T <= seg_row
     allowed = jnp.concatenate([allowed.astype(jnp.float32)] * GROUP, axis=1) > 0.5
@@ -215,9 +218,8 @@
         weights = jnp.exp(scores - jnp.max(scores, axis=0, keepdims=True))
         probs = (weights / jnp.sum(weights, axis=0, keepdims=True)).astype(jnp.bfloat16)
         vg[0:tokens, own] = jnp.dot(probs, g2, preferred_element_type=jnp.float32).astype(jnp.bfloat16)
-        if (j + 1) % heads_per_chunk == 0:
-            for n in (3, 1, 2, 0):
-                v_copy(j // heads_per_chunk, n).start()
+        if j + 1 == heads_per_chunk:
+            start_chunk(0)
 
     height = rows // SPLIT
 
@@ -240,14 +242,19 @@
                 total = (zs[m].astype(jnp.float32) + zb[m].astype(jnp.float32)).astype(jnp.bfloat16)
                 zt[m] = total
                 z_third(m).start()
-                gw_ref[band, step * k : step * (k + 1)] = total.astype(jnp.float32) * scale
+                gw_ref[band, step * k : step * (k + 1)] = total
 
     loads[5].wait()
+    for d in range(1, 8):
+        x_copy(d).wait_send()
+    start_chunk(1)
     for k in range(CHUNKS):
         columns = slice(step * k, step * (k + 1))
         for n in range(3):
             v_copy(k, n + 1).wait_recv()
             f_copy(k, n).start()
+        if k + 2 < CHUNKS:
+            start_chunk(k + 2)
         if k == 0:
             for d in range(1, 8):
                 x_copy(d).wait_recv()
@@ -297,7 +304,7 @@
         for k in range(CHUNKS):
             for m, band in pieces_of(k):
                 z_third(m).wait_recv()
-                gw_ref[band, step * k : step * (k + 1)] = za[m].astype(jnp.float32) * scale
+                gw_ref[band, step * k : step * (k + 1)] = za[m]
                 z_first(m).wait_send()
 
     @pl.when(jnp.logical_not(edge))
@@ -307,7 +314,6 @@
             z_third(m).wait_send()
 
     for d in range(1, 8):
-        x_copy(d).wait_send()
         g_copy(d).wait_send()
     for k in range(CHUNKS):
         for n in range(4):
@@ -326,11 +332,11 @@
     bf16 = jnp.bfloat16
     pieces = CHUNKS * SPLIT
     chunked = pltpu.VMEM((pieces, rows // SPLIT, step), bf16)
-    return pl.pallas_call(
-        functools.partial(fused_kernel, 1.0 / math.sqrt(tokens_all)),
+    grad_inputs, summed = pl.pallas_call(
+        fused_kernel,
         out_shape=(
             jax.ShapeDtypeStruct((tokens, features), bf16),
-            jax.ShapeDtypeStruct((rows, width), jnp.float32),
+            jax.ShapeDtypeStruct((rows, width), bf16),
         ),
         in_specs=[pl.BlockSpec(memory_space=pl.ANY)] * 6,
         out_specs=(pl.BlockSpec(memory_space=pltpu.VMEM),) * 2,
@@ -358,6 +364,7 @@
             collective_id=0, has_side_effects=True, vmem_limit_bytes=56 * 1024 * 1024
         ),
     )(inputs, queries, keys, grad_attn, segment_ids, value_weight)
+    return grad_inputs, summed.astype(jnp.float32) * (1.0 / math.sqrt(tokens_all))
 
 
 def plan(inputs, queries, keys, grad_attn, segment_ids, value_weight):

time: 48.9 us -> 48.1 us (0.984)
  other arithmetic: 0 us -> 2.28 us
  local copies, waits for them, and re-layouts: 3.03 us -> 0.82 us
  Pallas kernels: 45 us -> 44.2 us
    mul x0 -> x1, other arithmetic: none -> 2.28 us  [fused(): summed.astype(jnp.float32) * (1.0 / math.sqrt(tokens_all))]
    unnamed x4 -> x3, local copies, waits for them, and re-layouts: 3.03 us -> 0.82 us
    pallas_call x1, Pallas kernels: 45 us -> 44.2 us  [fused(): pl.pallas_call(fused_kernel, out_shape=(jax.ShapeDtypeStruct((tokens, fea...]
where the time goes in v3:
time: 48.1 us; the launch traced here: 47.9 us
  Pallas kernels  44.2 us (92%)
  other arithmetic  2.28 us (5%)
  local copies, waits for them, and re-layouts  0.82 us (2%)
  between operations  0.65 us (1%)
    pallas_call x1, Pallas kernels, fused(): pl.pallas_call(fused_kernel, out_shape=(jax.ShapeDtypeStruct((tokens, fea...  44.2 us
    mul x1, other arithmetic, fused(): summed.astype(jnp.float32) * (1.0 / math.sqrt(tokens_all))  2.28 us

profile of v3, /device:TPU:0, one launch (start us, length us, event | category | flops | bytes accessed | tf_op | source)
XLA Modules:
  0.0 47.9 jit_solution(2131269906311676859)
XLA Ops:
  0.6 44.2 %shard_map.77 = (bf16[128,2304]{1,0:T(8,128)(2,1)}, bf16[288,1024]{1,0:T(8,128)(2,1)}) custom-call(bf16[128,2304]{1,0:T(8,128)(2,1)} %x_hbm.1, bf16[128,2048]{1,0:T(8,128)(2,1)} %q_hbm.1, bf16[128,1024]{1,0:T(8,128)(2,1)} %k_hbm.1, bf16[128,2048]{1,0:T(8,128)(2,1)} %g_hbm.1, s32[1,128]{1,0:T(1,128)} %seg_hbm.1, bf16[288,1024]{1,0:T(8,128)(2,1)} %w_hbm.1), custom_call_target="tpu_custom_call" | custom-call | tf_op jit(solution)/shard_map/pallas_call | solution.py:335
  44.8 0.0 copy-start
  44.8 2.3 %convert_multiply_fusion = f32[288,1024]{1,0:T(8,128)} fusion(bf16[288,1024]{1,0:T(8,128)(2,1)} %get-tuple-element.5), kind=kLoop, calls=%fused_computation | loop fusion | flops 589824 | bytes 1769472 | tf_op jit(solution)/shard_map/mul | solution.py:367
  47.1 0.0 copy-done
  47.1 0.8 %copy.9 = bf16[128,2304]{1,0:T(8,128)(2,1)} copy(bf16[128,2304]{1,0:T(8,128)(2,1)S(1)} %copy-done) | data formatting | bytes 1179648
Async XLA Ops:
  44.8 2.3 %copy-start = (bf16[128,2304]{1,0:T(8,128)(2,1)S(1)}, bf16[128,2304]{1,0:T(8,128)(2,1)}, u32[]{:S(2)}) copy-start(bf16[128,2304]{1,0:T(8,128)(2,1)} %get-tuple-element.8) | copy-start | bytes 1769476

commit v4 on v3

--- a/solution.py
+++ b/solution.py
@@ -74,7 +74,7 @@
 
 
 CHUNKS = 4
-SPLIT = 3
+SPLIT = 6
 PAIRS = (6, 2, 4, 0)
 DIRECT = (1, 2, 4, 6)
 CROSS = (2, 4, 6)

time: 48.1 us -> 48.7 us (1.012)
  Pallas kernels: 44.2 us -> 44.8 us
    pallas_call x1, Pallas kernels: 44.2 us -> 44.8 us  [fused(): pl.pallas_call(fused_kernel, out_shape=(jax.ShapeDtypeStruct((tokens, fea...]
where the time goes in v4:
time: 48.7 us; the launch traced here: 48.5 us
  Pallas kernels  44.8 us (92%)
  other arithmetic  2.28 us (5%)
  local copies, waits for them, and re-layouts  0.82 us (2%)
  between operations  0.65 us (1%)
    pallas_call x1, Pallas kernels, fused(): pl.pallas_call(fused_kernel, out_shape=(jax.ShapeDtypeStruct((tokens, fea...  44.8 us
    mul x1, other arithmetic, fused(): summed.astype(jnp.float32) * (1.0 / math.sqrt(tokens_all))  2.28 us

profile of v4, /device:TPU:0, one launch (start us, length us, event | category | flops | bytes accessed | tf_op | source)
XLA Modules:
  0.0 48.5 jit_solution(5727156020536112184)
XLA Ops:
  0.6 44.8 %shard_map.77 = (bf16[128,2304]{1,0:T(8,128)(2,1)}, bf16[288,1024]{1,0:T(8,128)(2,1)}) custom-call(bf16[128,2304]{1,0:T(8,128)(2,1)} %x_hbm.1, bf16[128,2048]{1,0:T(8,128)(2,1)} %q_hbm.1, bf16[128,1024]{1,0:T(8,128)(2,1)} %k_hbm.1, bf16[128,2048]{1,0:T(8,128)(2,1)} %g_hbm.1, s32[1,128]{1,0:T(1,128)} %seg_hbm.1, bf16[288,1024]{1,0:T(8,128)(2,1)} %w_hbm.1), custom_call_target="tpu_custom_call" | custom-call | tf_op jit(solution)/shard_map/pallas_call | solution.py:335
  45.4 0.0 copy-start
  45.4 2.3 %convert_multiply_fusion = f32[288,1024]{1,0:T(8,128)} fusion(bf16[288,1024]{1,0:T(8,128)(2,1)} %get-tuple-element.5), kind=kLoop, calls=%fused_computation | loop fusion | flops 589824 | bytes 1769472 | tf_op jit(solution)/shard_map/mul | solution.py:367
  47.7 0.0 copy-done
  47.7 0.8 %copy.9 = bf16[128,2304]{1,0:T(8,128)(2,1)} copy(bf16[128,2304]{1,0:T(8,128)(2,1)S(1)} %copy-done) | data formatting | bytes 1179648
Async XLA Ops:
  45.4 2.3 %copy-start = (bf16[128,2304]{1,0:T(8,128)(2,1)S(1)}, bf16[128,2304]{1,0:T(8,128)(2,1)}, u32[]{:S(2)}) copy-start(bf16[128,2304]{1,0:T(8,128)(2,1)} %get-tuple-element.8) | copy-start | bytes 1769476
